TPU v7x, 256 devices: a whole 4x4x8 slice. The times are simulated.
256 devices in a mesh: ckpt: 8 (over z_lo, y), tensor: 8 (over z_hi, core), ex: 4 (over x).
Axes of the slice: x: 4, y: 4, z: 8 (z_hi: 4, z_lo: 2; z = z_hi * 2 + z_lo), core: 2. Of those that a mesh axis runs over, the one named last changes fastest.
Arguments:
- x_train: bfloat16 [8, 512, 5120], P('ckpt', ('tensor', 'ex')), may hold values from -6 to 6
- dy_train: bfloat16 [8, 512, 5120], P('ckpt', ('tensor', 'ex')), may hold values from -6 to 6
- x_test: bfloat16 [8, 512, 5120], P('ckpt', ('tensor', 'ex')), may hold values from -6 to 6
- dy_test: bfloat16 [8, 512, 5120], P('ckpt', ('tensor', 'ex')), may hold values from -6 to 6
- gate_train: bfloat16 [8, 512, 13824], P('ckpt', None, ('tensor', 'ex')), may hold values from -8 to 8
- gate_test: bfloat16 [8, 512, 13824], P('ckpt', None, ('tensor', 'ex')), may hold values from -8 to 8
- w_up: bfloat16 [8, 5120, 13824], P('ckpt', None, ('tensor', 'ex')), may hold values from -0.078125 to 0.078125
- w_down: bfloat16 [8, 13824, 5120], P('ckpt', ('tensor', 'ex')), may hold values from -0.078125 to 0.078125
- proj_hidden: int32 [13824, 64], P(('tensor', 'ex')), may hold values from 0 to 1
- proj_model: int32 [5120, 64], replicated, may hold values from 0 to 1
- rates: float32 [8], P('ckpt'), may hold values from 0.25 to 4
Outputs:
- scores: float32 [4, 4], P('ex')
All inputs are finite; a program needn't handle non-finite values.
Results may differ from a plain program's by a relative error of at most 0.0038.
Values may be sent and summed in bfloat16 or wider, within the bound.
No kernel may reach another device: no remote copies, remote signals or barrier semaphores. Data moves between devices by JAX's collectives and lax.ppermute only.
A program may use at most 128 MiB of HBM per device.

v0:
```python
import jax
import jax.numpy as jnp
from jax import lax
from jax.sharding import PartitionSpec as P

D = 5120
FF = 13824
KF = 64
KD = 64
SEQ = 128


def block_factors(x, dy, gate, w_up, w_down, sign_h, sign_m):
    up = jnp.dot(x, w_up, preferred_element_type=jnp.float32)
    act = jax.nn.silu(gate.astype(jnp.float32))
    hidden = (act * up).astype(jnp.bfloat16)
    grad_hidden = lax.dot_general(
        dy, w_down, (((1,), (1,)), ((), ())), preferred_element_type=jnp.float32
    )
    grad_up = (grad_hidden * act).astype(jnp.bfloat16)
    hidden_side = jnp.concatenate(
        [
            jnp.dot(hidden, sign_h, preferred_element_type=jnp.float32),
            jnp.dot(grad_up, sign_h, preferred_element_type=jnp.float32),
        ],
        axis=1,
    ) * FF ** (-0.5)
    model_side = jnp.concatenate(
        [
            jnp.dot(dy, sign_m, preferred_element_type=jnp.float32),
            jnp.dot(x, sign_m, preferred_element_type=jnp.float32),
        ],
        axis=1,
    ) * D ** (-0.5)
    return (hidden_side, model_side)


def sketch_rows(hidden_side, model_side):
    left = hidden_side.reshape(-1, SEQ, 2 * KF)
    right = model_side.reshape(-1, SEQ, 2 * KD)
    down = (
        jnp.einsum(
            "nsk,nsl->nkl", left[:, :, :KF], right[:, :, :KD], precision=lax.Precision.HIGHEST
        )
        / SEQ
    )
    upper = (
        jnp.einsum(
            "nsk,nsl->nkl", right[:, :, KD:], left[:, :, KF:], precision=lax.Precision.HIGHEST
        )
        / SEQ
    )
    count = left.shape[0]
    return jnp.concatenate([down.reshape(count, -1), upper.reshape(count, -1)], axis=1)


def body(
    x_train,
    dy_train,
    x_test,
    dy_test,
    gate_train,
    gate_test,
    w_up,
    w_down,
    proj_hidden,
    proj_model,
    rates,
):
    pieces = (x_train[0], dy_train[0], x_test[0], dy_test[0])
    gathered = (
        lax.all_gather(pieces[0], ("tensor", "ex"), axis=0, tiled=True),
        lax.all_gather(pieces[1], ("tensor", "ex"), axis=0, tiled=True),
        lax.all_gather(pieces[2], ("tensor", "ex"), axis=0, tiled=True),
        lax.all_gather(pieces[3], ("tensor", "ex"), axis=0, tiled=True),
    )
    train_x, train_dy, test_x, test_dy = gathered
    sign_h = (2 * proj_hidden - 1).astype(jnp.bfloat16)
    sign_m = (2 * proj_model - 1).astype(jnp.bfloat16)
    train_h, train_m = block_factors(
        train_x, train_dy, gate_train[0], w_up[0], w_down[0], sign_h, sign_m
    )
    test_h, test_m = block_factors(
        test_x, test_dy, gate_test[0], w_up[0], w_down[0], sign_h, sign_m
    )
    train_count = train_x.shape[0] // SEQ
    per_device = train_count // lax.axis_size("ex")
    start = lax.axis_index("ex") * per_device
    train_h, test_h = lax.psum((train_h, test_h), ("tensor", "ex"))
    train_sketch = sketch_rows(train_h, train_m)
    test_sketch = sketch_rows(test_h, test_m)
    mine = lax.dynamic_slice_in_dim(train_sketch, start, per_device, 0)
    block = rates[0] * jnp.dot(
        mine, test_sketch.T, precision=lax.Precision.HIGHEST, preferred_element_type=jnp.float32
    )
    return lax.psum(block, "ckpt")


def solution(mesh):
    in_specs = (
        P("ckpt", ("tensor", "ex"), None),
        P("ckpt", ("tensor", "ex"), None),
        P("ckpt", ("tensor", "ex"), None),
        P("ckpt", ("tensor", "ex"), None),
        P("ckpt", None, ("tensor", "ex")),
        P("ckpt", None, ("tensor", "ex")),
        P("ckpt", None, ("tensor", "ex")),
        P("ckpt", ("tensor", "ex"), None),
        P(("tensor", "ex"), None),
        P(),
        P("ckpt"),
    )
    out_specs = P("ex", None)
    return jax.shard_map(body, mesh=mesh, in_specs=in_specs, out_specs=out_specs, check_vma=False)
```

profile of v0, /device:TPU:2, one launch (start us, length us, event | category | flops | bytes accessed | tf_op | source)
XLA Modules:
  0.0 596.8 jit_solution(1330427506890708722)
XLA Ops:
  6.5 0.7 all-gather.9.cloned.1.call-update
  7.3 0.7 all-gather.11.cloned.1.call-update
  8.1 0.7 all-gather.13.cloned.1.call-update
  10.0 0.9 add_convert_fusion.1
  10.9 1.5 add_convert_fusion
  12.4 65.0 %all-gather.9.cloned.1.call-done = bf16[1,512,5120]{2,1,0:T(8,128)(2,1)} async-done(((bf16[1,16,5120]{2,1,0:T(8,128)(2,1)}), bf16[1,512,5120]{2,1,0:T(8,128)(2,1)}) %all-gather.9.cloned.1.call-update) | async-done | bytes 5242896 | tf_op jit(solution)/shard_map/all_gather | solution.py:72
  77.4 4.2 fusion.80
  81.6 60.7 %all-gather.11.cloned.1.call-done = bf16[1,512,5120]{2,1,0:T(8,128)(2,1)} async-done(((bf16[1,16,5120]{2,1,0:T(8,128)(2,1)}), bf16[1,512,5120]{2,1,0:T(8,128)(2,1)}) %all-gather.11.cloned.1.call-update) | async-done | bytes 5242896 | tf_op jit(solution)/shard_map/all_gather | solution.py:73
  142.3 4.2 fusion.83
  146.5 60.7 %all-gather.13.cloned.1.call-done = bf16[1,512,5120]{2,1,0:T(8,128)(2,1)} async-done(((bf16[1,16,5120]{2,1,0:T(8,128)(2,1)}), bf16[1,512,5120]{2,1,0:T(8,128)(2,1)}) %all-gather.13.cloned.1.call-update) | async-done | bytes 5242896 | tf_op jit(solution)/shard_map/all_gather | solution.py:74
  207.3 4.2 fusion.86
  211.5 6.5 %fusion.62 = f32[512,64]{0,1:T(8,128)S(1)} fusion(bf16[432,64]{0,1:T(8,128)(2,1)S(1)} %add_convert_fusion.1, bf16[1,5120,432]{1,2,0:T(8,128)(2,1)} %param.17, bf16[1,512,5120]{2,1,0:T(8,128)(2,1)} %all-gather.9.cloned.1.call-done, bf16[1,512,432]{1,2,0:T(8,128)(2,1)S(1)} %copy-done), kind=kOutput, calls=%fused_computation.29 | convolution fusion | flops 2294784000 | bytes 10295296 | tf_op jit(solution)/shard_map/dot_general | solution.py:23
  218.0 6.7 %fusion.67 = f32[512,64]{0,1:T(8,128)S(1)} fusion(bf16[432,64]{0,1:T(8,128)(2,1)S(1)} %add_convert_fusion.1, bf16[1,432,5120]{2,1,0:T(8,128)(2,1)} %param.18, bf16[1,512,5120]{2,1,0:T(8,128)(2,1)} %all-gather.11.cloned.1.call-done, bf16[1,512,432]{1,2,0:T(8,128)(2,1)S(1)} %copy-done), kind=kOutput, calls=%fused_computation.30 | convolution fusion | flops 2294784000 | bytes 10295296 | tf_op jit(solution)/shard_map/dot_general | solution.py:24
  224.8 6.6 %fusion.72 = f32[512,64]{0,1:T(8,128)S(1)} fusion(bf16[432,64]{0,1:T(8,128)(2,1)S(1)} %add_convert_fusion.1, bf16[1,5120,432]{1,2,0:T(8,128)(2,1)} %param.17, bf16[1,512,5120]{2,1,0:T(8,128)(2,1)} %all-gather.13.cloned.1.call-done, bf16[1,512,432]{1,2,0:T(8,128)(2,1)S(1)} %copy-done.1), kind=kOutput, calls=%fused_computation.31 | convolution fusion | flops 2294784000 | bytes 10295296 | tf_op jit(solution)/shard_map/dot_general | solution.py:23
  231.3 40.7 %all-gather.15.cloned.1.call-done = bf16[1,512,5120]{2,1,0:T(8,128)(2,1)} async-done(((bf16[1,16,5120]{2,1,0:T(8,128)(2,1)}), bf16[1,512,5120]{2,1,0:T(8,128)(2,1)}) %all-gather.15.cloned.1.call-update) | async-done | bytes 5242896 | tf_op jit(solution)/shard_map/all_gather | solution.py:75
  272.1 6.7 %fusion.77 = f32[512,64]{0,1:T(8,128)S(1)} fusion(bf16[432,64]{0,1:T(8,128)(2,1)S(1)} %add_convert_fusion.1, bf16[1,432,5120]{2,1,0:T(8,128)(2,1)} %param.18, bf16[1,512,5120]{2,1,0:T(8,128)(2,1)} %all-gather.15.cloned.1.call-done, bf16[1,512,432]{1,2,0:T(8,128)(2,1)S(1)} %copy-done.1), kind=kOutput, calls=%fused_computation.32 | convolution fusion | flops 2294784000 | bytes 10295296 | tf_op jit(solution)/shard_map/dot_general | solution.py:24
  278.8 0.9 copy_bitcast_fusion
  279.7 4.2 fusion.89
  283.9 280.9 %all-reduce.3.cloned.1.call-done = (f32[4,128,128]{1,2,0:T(8,128)}, f32[4,128,128]{1,2,0:T(8,128)}) async-done(((f32[4,128,128]{1,2,0:T(8,128)}, f32[4,128,128]{1,2,0:T(8,128)}), (f32[4,128,128]{1,2,0:T(8,128)}, f32[4,128,128]{1,2,0:T(8,128)})) %all-reduce.3.cloned.1.call-update) | async-done | bytes 524304 | tf_op jit(solution)/shard_map/psum | solution.py:89
  564.8 1.2 convolution_multiply_fusion.3
  566.1 1.2 convolution_multiply_fusion.2
  567.3 1.2 convolution_multiply_fusion.1
  568.6 1.2 convolution_multiply_fusion
  570.9 19.3 %psum.23 = f32[1,4]{1,0:T(1,128)} all-reduce(f32[1,4]{1,0:T(1,128)S(1)} %fusion.93), channel_id=1, replica_groups=mesh['ckpt'=8,'tensor'=8,'ex'=4] {'ckpt'}, use_global_device_ids=true, to_apply=%region_2.3 | all-reduce | flops 4 | bytes 32 | tf_op jit(solution)/shard_map/psum | solution.py:96
  (22 shorter events, 1.9 us)
Async XLA Ops:
  6.5 70.8 %all-gather.9.cloned.1.call-start = ((), (), s32[]{:S(2)}) async-start(), calls=%async_computation | async-start | bytes 5406720 | tf_op jit(solution)/shard_map/all_gather | solution.py:72
  7.3 135.1 %all-gather.11.cloned.1.call-start = ((), (), s32[]{:S(2)}) async-start(), calls=%async_computation.1 | async-start | bytes 5406720 | tf_op jit(solution)/shard_map/all_gather | solution.py:73
  8.0 199.3 %all-gather.13.cloned.1.call-start = ((), (), s32[]{:S(2)}) async-start(), calls=%async_computation.2 | async-start | bytes 5406720 | tf_op jit(solution)/shard_map/all_gather | solution.py:74
  8.7 263.3 %all-gather.15.cloned.1.call-start = ((), (), s32[]{:S(2)}) async-start(), calls=%async_computation.3 | async-start | bytes 5406720 | tf_op jit(solution)/shard_map/all_gather | solution.py:75
  9.3 555.5 %all-reduce.3.cloned.1.call-start = ((), (), s32[]{:S(2)}) async-start(), calls=%async_computation.4 | async-start | bytes 1048576 | tf_op jit(solution)/shard_map/psum | solution.py:89
  81.6 129.9 %copy-start = (bf16[1,512,432]{1,2,0:T(8,128)(2,1)S(1)}, bf16[1,512,432]{1,2,0:T(8,128)(2,1)}, u32[]{:S(2)}) copy-start(bf16[1,512,432]{1,2,0:T(8,128)(2,1)} %param.15) | copy-start | bytes 1327108
  218.0 6.7 %copy-start.1 = (bf16[1,512,432]{1,2,0:T(8,128)(2,1)S(1)}, bf16[1,512,432]{1,2,0:T(8,128)(2,1)}, u32[]{:S(2)}) copy-start(bf16[1,512,432]{1,2,0:T(8,128)(2,1)} %param.16) | copy-start | bytes 1327108
Sparse Core Ops, SparseCore 0:
  9.9 67.4 all-gather.8
  79.9 62.3 all-gather.10
  144.9 62.3 all-gather.12
  209.7 62.3 all-gather.14
  279.8 284.9 all-reduce.2
where the time goes:
time: 597 us
  waiting for transfers between devices  511 us (86%)
  matrix products  49 us (8%)
  blocking collectives  19.3 us (3%)
  between operations  13.9 us (2%)
    psum x1, waiting for transfers between devices, body(): train_h, test_h = lax.psum((train_h, test_h), ('tensor', 'ex'))  281 us
    all_gather x1, waiting for transfers between devices, body(): lax.all_gather(pieces[0], ('tensor', 'ex'), axis=0, tiled=True)  65 us
    all_gather x1, waiting for transfers between devices, body(): lax.all_gather(pieces[2], ('tensor', 'ex'), axis=0, tiled=True)  60.7 us
    all_gather x1, waiting for transfers between devices, body(): lax.all_gather(pieces[1], ('tensor', 'ex'), axis=0, tiled=True)  60.7 us
    all_gather x1, waiting for transfers between devices, body(): lax.all_gather(pieces[3], ('tensor', 'ex'), axis=0, tiled=True)  40.7 us
    psum x1, blocking collectives, body(): return lax.psum(block, 'ckpt')  19.3 us
    dot_general x2, matrix products, block_factors(): jnp.dot(grad_up, sign_h, preferred_element_type=jnp.float32)  13.4 us
    dot_general x2, matrix products, block_factors(): jnp.dot(hidden, sign_h, preferred_element_type=jnp.float32)  13.1 us
  transfers between devices with their start and end apart: 5, of which 5 were waited for; matrix products, arithmetic and copies ran while one was open for 7% of the time, Pallas kernels for 0%

commit v1 on v0

--- a/solution.py
+++ b/solution.py
@@ -86,7 +86,7 @@
     train_count = train_x.shape[0] // SEQ
     per_device = train_count // lax.axis_size("ex")
     start = lax.axis_index("ex") * per_device
-    train_h, test_h = lax.psum((train_h, test_h), ("tensor", "ex"))
+    train_h, test_h = lax.psum(lax.psum((train_h, test_h), "ex"), "tensor")
     train_sketch = sketch_rows(train_h, train_m)
     test_sketch = sketch_rows(test_h, test_m)
     mine = lax.dynamic_slice_in_dim(train_sketch, start, per_device, 0)

time: 597 us -> 435 us (0.73)
  waiting for transfers between devices: 511 us -> 346 us
    psum x1 -> x2, waiting for transfers between devices: 281 us -> 104 us  [body(): train_h, test_h = lax.psum(lax.psum((train_h, test_h), 'ex'), 'tensor')]
    all_gather x1, waiting for transfers between devices: 40.7 us -> 58.3 us  [body(): lax.all_gather(pieces[3], ('tensor', 'ex'), axis=0, tiled=True)]
  transfers between devices with their start and end apart: 5 -> 6, of which waited for: 5 -> 6; matrix products, arithmetic and copies ran while one was open for 7% -> 9% of each run, Pallas kernels for 0% -> 0%
where the time goes in v1:
time: 435 us
  waiting for transfers between devices  346 us (80%)
  matrix products  48.5 us (11%)
  blocking collectives  19.2 us (4%)
  between operations  14.2 us (3%)
    psum x2, waiting for transfers between devices, body(): train_h, test_h = lax.psum(lax.psum((train_h, test_h), 'ex'), 'tensor')  104 us
    all_gather x1, waiting for transfers between devices, body(): lax.all_gather(pieces[0], ('tensor', 'ex'), axis=0, tiled=True)  64.9 us
    all_gather x1, waiting for transfers between devices, body(): lax.all_gather(pieces[1], ('tensor', 'ex'), axis=0, tiled=True)  58.4 us
    all_gather x1, waiting for transfers between devices, body(): lax.all_gather(pieces[3], ('tensor', 'ex'), axis=0, tiled=True)  58.3 us
    all_gather x1, waiting for transfers between devices, body(): lax.all_gather(pieces[2], ('tensor', 'ex'), axis=0, tiled=True)  57.7 us
    psum x1, blocking collectives, body(): return lax.psum(block, 'ckpt')  19.2 us
    dot_general x2, matrix products, block_factors(): jnp.dot(hidden, sign_h, preferred_element_type=jnp.float32)  13 us
    dot_general x2, matrix products, block_factors(): jnp.dot(grad_up, sign_h, preferred_element_type=jnp.float32)  13 us
  transfers between devices with their start and end apart: 6, of which 6 were waited for; matrix products, arithmetic and copies ran while one was open for 9% of the time, Pallas kernels for 0%

profile of v1, /device:TPU:2, one launch (start us, length us, event | category | flops | bytes accessed | tf_op | source)
XLA Modules:
  0.0 435.0 jit_solution(922996600056908757)
XLA Ops:
  10.0 0.9 add_convert_fusion.1
  10.9 1.5 add_convert_fusion
  12.4 64.9 %all-gather.9.cloned.1.call-done = bf16[1,512,5120]{2,1,0:T(8,128)(2,1)} async-done(((bf16[1,16,5120]{2,1,0:T(8,128)(2,1)}), bf16[1,512,5120]{2,1,0:T(8,128)(2,1)}) %all-gather.9.cloned.1.call-update) | async-done | bytes 5242896 | tf_op jit(solution)/shard_map/all_gather | solution.py:72
  77.4 6.5 %fusion.62 = f32[512,64]{0,1:T(8,128)S(1)} fusion(bf16[432,64]{0,1:T(8,128)(2,1)S(1)} %add_convert_fusion.1, bf16[1,5120,432]{1,2,0:T(8,128)(2,1)} %param.17, bf16[1,512,5120]{2,1,0:T(8,128)(2,1)} %all-gather.9.cloned.1.call-done, bf16[1,512,432]{1,2,0:T(8,128)(2,1)} %param.15), kind=kOutput, calls=%fused_computation.29 | convolution fusion | flops 2294784000 | bytes 10295296 | tf_op jit(solution)/shard_map/dot_general | solution.py:23
  83.9 58.4 %all-gather.11.cloned.1.call-done = bf16[1,512,5120]{2,1,0:T(8,128)(2,1)} async-done(((bf16[1,16,5120]{2,1,0:T(8,128)(2,1)}), bf16[1,512,5120]{2,1,0:T(8,128)(2,1)}) %all-gather.11.cloned.1.call-update) | async-done | bytes 5242896 | tf_op jit(solution)/shard_map/all_gather | solution.py:73
  142.3 6.5 %fusion.67 = f32[512,64]{0,1:T(8,128)S(1)} fusion(bf16[432,64]{0,1:T(8,128)(2,1)S(1)} %add_convert_fusion.1, bf16[1,432,5120]{2,1,0:T(8,128)(2,1)} %param.18, bf16[1,512,5120]{2,1,0:T(8,128)(2,1)} %all-gather.11.cloned.1.call-done, bf16[1,512,432]{1,2,0:T(8,128)(2,1)S(1)} %copy-done), kind=kOutput, calls=%fused_computation.30 | convolution fusion | flops 2294784000 | bytes 10295296 | tf_op jit(solution)/shard_map/dot_general | solution.py:24
  148.8 0.8 maximum_multiply_fusion
  149.6 57.7 %all-gather.13.cloned.1.call-done = bf16[1,512,5120]{2,1,0:T(8,128)(2,1)} async-done(((bf16[1,16,5120]{2,1,0:T(8,128)(2,1)}), bf16[1,512,5120]{2,1,0:T(8,128)(2,1)}) %all-gather.13.cloned.1.call-update) | async-done | bytes 5242896 | tf_op jit(solution)/shard_map/all_gather | solution.py:74
  207.3 6.5 %fusion.72 = f32[512,64]{0,1:T(8,128)S(1)} fusion(bf16[432,64]{0,1:T(8,128)(2,1)S(1)} %add_convert_fusion.1, bf16[1,5120,432]{1,2,0:T(8,128)(2,1)} %param.17, bf16[1,512,5120]{2,1,0:T(8,128)(2,1)} %all-gather.13.cloned.1.call-done, bf16[1,512,432]{1,2,0:T(8,128)(2,1)S(1)} %copy-done.1), kind=kOutput, calls=%fused_computation.31 | convolution fusion | flops 2294784000 | bytes 10295296 | tf_op jit(solution)/shard_map/dot_general | solution.py:23
  213.8 58.3 %all-gather.15.cloned.1.call-done = bf16[1,512,5120]{2,1,0:T(8,128)(2,1)} async-done(((bf16[1,16,5120]{2,1,0:T(8,128)(2,1)}), bf16[1,512,5120]{2,1,0:T(8,128)(2,1)}) %all-gather.15.cloned.1.call-update) | async-done | bytes 5242896 | tf_op jit(solution)/shard_map/all_gather | solution.py:75
  272.1 6.5 %fusion.77 = f32[512,64]{0,1:T(8,128)S(1)} fusion(bf16[432,64]{0,1:T(8,128)(2,1)S(1)} %add_convert_fusion.1, bf16[1,432,5120]{2,1,0:T(8,128)(2,1)} %param.18, bf16[1,512,5120]{2,1,0:T(8,128)(2,1)} %all-gather.15.cloned.1.call-done, bf16[1,512,432]{1,2,0:T(8,128)(2,1)S(1)} %copy-done.1), kind=kOutput, calls=%fused_computation.32 | convolution fusion | flops 2294784000 | bytes 10295296 | tf_op jit(solution)/shard_map/dot_general | solution.py:24
  278.6 0.7 maximum_multiply_fusion.2
  279.6 4.2 fusion.80
  283.8 4.2 fusion.83
  288.0 4.2 fusion.86
  292.2 32.3 %all-reduce.7.cloned.1.call-done = (f32[512,128]{0,1:T(8,128)}, f32[512,128]{0,1:T(8,128)}) async-done(((f32[512,128]{0,1:T(8,128)}, f32[512,128]{0,1:T(8,128)}), (f32[512,128]{0,1:T(8,128)}, f32[512,128]{0,1:T(8,128)})) %all-reduce.7.cloned.1.call-update) | async-done | bytes 524304 | tf_op jit(solution)/shard_map/psum | solution.py:89
  324.6 1.9 copy_bitcast_fusion
  326.5 4.2 fusion.89
  330.8 72.1 %all-reduce.5.cloned.1.call-done = (f32[4,128,128]{1,2,0:T(8,128)}, f32[4,128,128]{1,2,0:T(8,128)}) async-done(((f32[4,128,128]{1,2,0:T(8,128)}, f32[4,128,128]{1,2,0:T(8,128)}), (f32[4,128,128]{1,2,0:T(8,128)}, f32[4,128,128]{1,2,0:T(8,128)})) %all-reduce.5.cloned.1.call-update) | async-done | bytes 524304 | tf_op jit(solution)/shard_map/psum | solution.py:89
  402.9 1.2 convolution_multiply_fusion.3
  404.1 1.2 convolution_multiply_fusion.2
  405.4 1.2 convolution_multiply_fusion.1
  406.6 1.2 convolution_multiply_fusion
  409.0 19.2 %psum.39 = f32[1,4]{1,0:T(1,128)} all-reduce(f32[1,4]{1,0:T(1,128)S(1)} %fusion.93), channel_id=1, replica_groups=mesh['ckpt'=8,'tensor'=8,'ex'=4] {'ckpt'}, use_global_device_ids=true, to_apply=%region_4.5 | all-reduce | flops 4 | bytes 32 | tf_op jit(solution)/shard_map/psum | solution.py:96
  (27 shorter events, 4.2 us)
Async XLA Ops:
  6.5 70.8 %all-gather.9.cloned.1.call-start = ((), (), s32[]{:S(2)}) async-start(), calls=%async_computation | async-start | bytes 5406720 | tf_op jit(solution)/shard_map/all_gather | solution.py:72
  7.3 135.1 %all-gather.11.cloned.1.call-start = ((), (), s32[]{:S(2)}) async-start(), calls=%async_computation.1 | async-start | bytes 5406720 | tf_op jit(solution)/shard_map/all_gather | solution.py:73
  8.0 199.3 %all-gather.13.cloned.1.call-start = ((), (), s32[]{:S(2)}) async-start(), calls=%async_computation.2 | async-start | bytes 5406720 | tf_op jit(solution)/shard_map/all_gather | solution.py:74
  8.7 263.3 %all-gather.15.cloned.1.call-start = ((), (), s32[]{:S(2)}) async-start(), calls=%async_computation.3 | async-start | bytes 5406720 | tf_op jit(solution)/shard_map/all_gather | solution.py:75
  9.3 315.3 %all-reduce.7.cloned.1.call-start = ((), (), s32[]{:S(2)}) async-start(), calls=%async_computation.5 | async-start | bytes 1048576 | tf_op jit(solution)/shard_map/psum | solution.py:89
  12.4 129.9 %copy-start = (bf16[1,512,432]{1,2,0:T(8,128)(2,1)S(1)}, bf16[1,512,432]{1,2,0:T(8,128)(2,1)}, u32[]{:S(2)}) copy-start(bf16[1,512,432]{1,2,0:T(8,128)(2,1)} %param.15) | copy-start | bytes 1327108
  83.9 123.4 %copy-start.1 = (bf16[1,512,432]{1,2,0:T(8,128)(2,1)S(1)}, bf16[1,512,432]{1,2,0:T(8,128)(2,1)}, u32[]{:S(2)}) copy-start(bf16[1,512,432]{1,2,0:T(8,128)(2,1)} %param.16) | copy-start | bytes 1327108
  279.3 123.5 %all-reduce.5.cloned.1.call-start = ((), (), s32[]{:S(2)}) async-start(), calls=%async_computation.4 | async-start | bytes 1048576 | tf_op jit(solution)/shard_map/psum | solution.py:89
Sparse Core Ops, SparseCore 0:
  9.9 67.4 all-gather.8
  79.9 62.3 all-gather.10
  144.9 62.3 all-gather.12
  209.7 62.3 all-gather.14
  279.5 45.0 all-reduce.6
  327.1 75.7 all-reduce.4
